TPU v7x, 32 devices: a whole 2x2x4 slice. The times are simulated.
32 devices in a mesh: groups: 2 (over x), row: 8 (over z, y), col: 2 (over core).
Axes of the slice: x: 2, y: 2, z: 4, core: 2. Of those that a mesh axis runs over, the one named last changes fastest.
Arguments:
- points: float32 [32768, 128], P(('groups', 'row', 'col')), parts along dimension 0, may hold values from -8 to 8, as said below
- start: float32 [32768, 64], P(('groups', 'row', 'col')), parts along dimension 0, may hold values from -6 to 6
- pair_mask: int32 [32, 7], P(('groups', 'row', 'col')), parts along dimension 0, may hold values from 0 to 1, as said below
Outputs:
- embedding: float32 [32768, 64], P(('groups', 'row', 'col')), parts along dimension 0
- degree: float32 [32768], P(('groups', 'row', 'col')), parts along dimension 0
There are 2 independent parts, one for each index of `groups`. A program takes and returns all parts, laid end to end along the dimension named above; each array names one. Nothing has to cross between parts.
Inputs may be any that keep to these rules, and one draw needn't show every extreme that they name: pair_mask[b, d - 1] is 1 where block b pairs with block b + d, and 0 wherever b + d >= 16; blocks differ in how many partners they have. `points`: independent features of order one.
All inputs are finite; a program needn't handle non-finite values.
Results may differ from a plain program's by a relative error of at most 0.0042.
Values may be sent and summed in bfloat16 or wider, within the bound.
A program may use at most 64 MiB of HBM per device.

v0:
```python
import functools
import math

import jax
import jax.numpy as jnp
from jax import lax
from jax.experimental import pallas as pl
from jax.experimental.pallas import tpu as pltpu
from jax.sharding import PartitionSpec as P

STEPS = 2
MESH = pl.DeviceIdType.MESH
PAD = 16


def inverse_cholesky(gram):
    n = gram.shape[0]
    rows = lax.broadcasted_iota(jnp.int32, (n, 2 * n), 0)
    lanes = lax.broadcasted_iota(jnp.int32, (n, 2 * n), 1)
    eye = jnp.where(lanes == rows + n, 1.0, 0.0)
    mat = jnp.concatenate([gram, jnp.zeros_like(gram)], axis=1) + eye
    diag = jnp.ones((n, 1), jnp.float32)
    row_of = lax.broadcasted_iota(jnp.int32, (n, 1), 0)
    for k in range(n):
        pivot = mat[k:k + 1, k:k + 1]
        diag = jnp.where(row_of == k, pivot, diag)
        if k < n - 1:
            line = mat[k:k + 1, :] * (1.0 / pivot)
            column = jnp.where(row_of > k, mat[:, k:k + 1], 0.0)
            mat = mat - column * line
    return mat[:, n:] * lax.rsqrt(diag)


def kernel(rows_n, span, points_ref, start_ref, mask_ref, out_ref, degree_ref,
           pts, near_t, tiles, emb, acc, y_t, gram, gram_near, gram_all, gram_sum,
           pts_send, pts_recv, emb_send, emb_recv, gsend, grecv, gall_send, gall_recv):
    group = lax.axis_index("groups")
    chip = lax.axis_index("row")
    core = lax.axis_index("col")
    mine = 2 * chip + core
    total = 2 * rows_n
    other = 1 - core
    side = 1 - 2 * core
    blk = points_ref.shape[0]
    width = start_ref.shape[1]
    feats = points_ref.shape[1]
    reach = span // 2
    c2 = 4.0 / feats * math.log2(math.e)

    far_chip = chip + (reach + 1) * (2 * core - 1)
    has_far = jnp.logical_and(far_chip >= 0, far_chip < rows_n)

    barrier = pltpu.get_barrier_semaphore()

    def greet(o, _):
        pl.semaphore_signal(barrier, inc=1, device_id=(group, lax.rem(chip + o, rows_n), core), device_id_type=MESH)
        return 0

    lax.fori_loop(1, rows_n, greet, 0)
    pl.semaphore_signal(barrier, inc=1, device_id=(group, chip, other), device_id_type=MESH)

    @pl.when(has_far)
    def _():
        pl.semaphore_signal(barrier, inc=1, device_id=(group, far_chip, other), device_id_type=MESH)

    pts[span, 0:blk, :] = points_ref[...].astype(jnp.bfloat16)
    lane = lax.broadcasted_iota(jnp.int32, (PAD, feats), 1)
    flags = jnp.where(lane == feats - 1, 1.0, 0.0)
    for i in range(span):
        flags = jnp.where(lane == i, mask_ref[0, i].astype(jnp.float32), flags)
    pts[span, blk:blk + PAD, :] = flags.astype(jnp.bfloat16)

    pl.semaphore_wait(barrier, rows_n + has_far.astype(jnp.int32))

    def send_to(buf, send, recv, from_slot, to_slot, sem, to_chip, to_core):
        return pltpu.make_async_remote_copy(
            src_ref=buf.at[from_slot], dst_ref=buf.at[to_slot],
            send_sem=send.at[sem], recv_sem=recv.at[to_slot],
            device_id=(group, to_chip, to_core), device_id_type=MESH)

    def own_sends(buf, send, recv, action):
        def near(apart):
            @pl.when(jnp.logical_and(chip + apart >= 0, chip + apart < rows_n))
            def _():
                action(send_to(buf, send, recv, span, span - 2 * apart, span + 2 * apart, chip + apart, core))

        action(send_to(buf, send, recv, span, span - side, span, chip, other))
        for apart in range(1, reach + 1):
            near(apart)
            near(-apart)

        @pl.when(has_far)
        def _():
            action(send_to(buf, send, recv, span, span - span * (2 * core - 1), 2 * span + 1, far_chip, other))

    def relay(buf, send, recv, d):
        return send_to(buf, send, recv, span + d, span + d - side, span + d + 1, chip, other)

    def exchange(buf, send, recv, use):
        own_sends(buf, send, recv, lambda copy: copy.start())

        def turn(t, _):
            g = (t + 3) // 4 - 1 + (t == 0).astype(jnp.int32)
            r = (t + 3) % 4
            size = jnp.minimum(jnp.where(r < 2, 2 * g + 2, 2 * g + 1), span)
            d = jnp.where(t == 0, 0, jnp.where(r % 2 == 0, size, -size))
            valid = jnp.logical_and(mine + d >= 0, mine + d < total)

            @pl.when(jnp.logical_and(valid, d != 0))
            def _():
                send_to(buf, send, recv, span + d, span + d, 0, chip, other).wait_recv()

                @pl.when(size % 2 == 0)
                def _():
                    relay(buf, send, recv, d).start()

            @pl.when(valid)
            def _():
                use(d)
            return 0

        lax.fori_loop(0, 2 * span + 1, turn, 0)

    def finish(buf, send, recv):
        own_sends(buf, send, recv, lambda copy: copy.wait_send())
        for apart in range(1, reach + 1):
            for d in (2 * apart, -2 * apart):
                @pl.when(jnp.logical_and(mine + d >= 0, mine + d < total))
                def _(d=d):
                    relay(buf, send, recv, d).wait_send()

    near_f = pts[span, 0:blk, :].astype(jnp.float32).T
    near_t[...] = near_f.astype(jnp.bfloat16)
    near_sq = -c2 * jnp.sum(near_f * near_f, axis=0, keepdims=True)
    degree_ref[...] = jnp.zeros_like(degree_ref)
    step = 128

    def make_tile(d):
        flag_row = pts[span + jnp.minimum(d, 0), blk:blk + PAD, :].astype(jnp.float32)
        which = jnp.where(d == 0, feats - 1, jnp.abs(d) - 1)
        live = jnp.sum(jnp.where(lane == which, flag_row, 0.0)[0:1], axis=1, keepdims=True)
        near_term = near_sq + (1.0 - live) * -1.0e4

        def part(i, sums):
            at = pl.ds(pl.multiple_of(i * step, step), step)
            far = pts[span + d, at, :]
            far_f = far.astype(jnp.float32)
            far_sq = -c2 * jnp.sum(far_f * far_f, axis=1, keepdims=True)
            inner = jnp.dot(far, near_t[...], preferred_element_type=jnp.float32)
            tile = jnp.exp2((2.0 * c2) * inner + far_sq + near_term).astype(jnp.bfloat16)
            tiles[span + d, at, :] = tile
            return sums + jnp.sum(tile.astype(jnp.float32), axis=0, keepdims=True)

        degree_ref[...] += lax.fori_loop(0, blk // step, part, jnp.zeros((1, blk), jnp.float32))

    exchange(pts, pts_send, pts_recv, make_tile)
    inverse_root = lax.rsqrt(degree_ref[...])
    current = start_ref[...].T

    for it in range(STEPS):
        ebuf, esend, erecv = emb.at[it], emb_send.at[it], emb_recv.at[it]
        ebuf[span] = (inverse_root * current).astype(jnp.bfloat16)
        acc[...] = jnp.zeros_like(acc)

        def product(d):
            acc[...] += jnp.dot(ebuf[span + d], tiles[span + d], preferred_element_type=jnp.float32)

        exchange(ebuf, esend, erecv, product)
        y_t[...] = inverse_root * acc[...]
        local = lax.dot_general(y_t[...], y_t[...], (((1,), (1,)), ((), ())),
                                precision=lax.Precision.HIGHEST, preferred_element_type=jnp.float32)
        half = width // 2
        quarter = half // 2
        gram[it] = jnp.concatenate([local[0:half], local[half:width]], axis=1)
        own = pl.ds(pl.multiple_of(core * quarter, quarter), quarter)
        its = pl.ds(pl.multiple_of(other * quarter, quarter), quarter)
        first = pltpu.make_async_remote_copy(
            src_ref=gram.at[it, its], dst_ref=gram_near.at[it],
            send_sem=gsend.at[it, 0], recv_sem=grecv.at[it, 0],
            device_id=(group, chip, other), device_id_type=MESH)
        first.start()
        first.wait_recv()
        gram_all[it, chip] = gram[it, own] + gram_near[it]

        def scatter(o):
            to = lax.rem(chip + o, rows_n)
            return pltpu.make_async_remote_copy(
                src_ref=gram_all.at[it, chip], dst_ref=gram_all.at[it, chip],
                send_sem=gall_send.at[it, o], recv_sem=gall_recv.at[it, chip],
                device_id=(group, to, core), device_id_type=MESH)

        def start_one(o, _):
            scatter(o).start()
            return 0

        lax.fori_loop(1, rows_n, start_one, 0)

        def await_one(o, _):
            source = lax.rem(chip + o, rows_n)
            pltpu.make_async_remote_copy(
                src_ref=gram_all.at[it, source], dst_ref=gram_all.at[it, source],
                send_sem=gall_send.at[it, o], recv_sem=gall_recv.at[it, source],
                device_id=(group, source, core), device_id_type=MESH).wait_recv()
            return 0

        lax.fori_loop(1, rows_n, await_one, 0)
        gram_sum[it, own] = jnp.sum(gram_all[it], axis=0)
        last = pltpu.make_async_remote_copy(
            src_ref=gram_sum.at[it, own], dst_ref=gram_sum.at[it, own],
            send_sem=gsend.at[it, 1], recv_sem=grecv.at[it, 1],
            device_id=(group, chip, other), device_id_type=MESH)
        last.start()
        last.wait_recv()
        packed = gram_sum[it] * (1.0 / (blk * total))
        whole = jnp.concatenate([packed[:, 0:width], packed[:, width:2 * width]], axis=0)
        current = jnp.dot(inverse_cholesky(whole), y_t[...],
                          precision=lax.Precision.HIGHEST, preferred_element_type=jnp.float32)
        first.wait_send()
        last.wait_send()

        def sent_one(o, _):
            scatter(o).wait_send()
            return 0

        lax.fori_loop(1, rows_n, sent_one, 0)

    out_ref[...] = current.T
    finish(pts, pts_send, pts_recv)
    for it in range(STEPS):
        finish(emb.at[it], emb_send.at[it], emb_recv.at[it])


def per_device(rows_n, points, start, pair_mask):
    blk, feats = points.shape
    width = start.shape[1]
    span = pair_mask.shape[1]
    slots = 2 * span + 1
    vmem = pl.BlockSpec(memory_space=pltpu.VMEM)
    embedding, degree = pl.pallas_call(
        functools.partial(kernel, rows_n, span),
        out_shape=(jax.ShapeDtypeStruct((blk, width), jnp.float32), jax.ShapeDtypeStruct((1, blk), jnp.float32)),
        in_specs=[vmem, vmem, pl.BlockSpec(memory_space=pltpu.SMEM)],
        out_specs=(vmem, vmem),
        scratch_shapes=[
            pltpu.VMEM((slots, blk + PAD, feats), jnp.bfloat16),
            pltpu.VMEM((feats, blk), jnp.bfloat16),
            pltpu.VMEM((slots, blk, blk), jnp.bfloat16),
            pltpu.VMEM((STEPS, slots, width, blk), jnp.bfloat16),
            pltpu.VMEM((width, blk), jnp.float32),
            pltpu.VMEM((width, blk), jnp.float32),
            pltpu.VMEM((STEPS, width // 2, 2 * width), jnp.float32),
            pltpu.VMEM((STEPS, width // 4, 2 * width), jnp.float32),
            pltpu.VMEM((STEPS, rows_n, width // 4, 2 * width), jnp.float32),
            pltpu.VMEM((STEPS, width // 2, 2 * width), jnp.float32),
            pltpu.SemaphoreType.DMA((slots + 1,)),
            pltpu.SemaphoreType.DMA((slots,)),
            pltpu.SemaphoreType.DMA((STEPS, slots + 1)),
            pltpu.SemaphoreType.DMA((STEPS, slots)),
            pltpu.SemaphoreType.DMA((STEPS, 2)),
            pltpu.SemaphoreType.DMA((STEPS, 2)),
            pltpu.SemaphoreType.DMA((STEPS, rows_n)),
            pltpu.SemaphoreType.DMA((STEPS, rows_n)),
        ],
        compiler_params=pltpu.CompilerParams(
            collective_id=0, has_side_effects=True, vmem_limit_bytes=56 * 1024 * 1024),
    )(points, start, pair_mask)
    return embedding, degree[0]


def solution(mesh):
    rows = P(("groups", "row", "col"), None)
    return jax.shard_map(
        functools.partial(per_device, mesh.shape["row"]), mesh=mesh, in_specs=(rows, rows, rows),
        out_specs=(rows, P(("groups", "row", "col"))), check_vma=False)
```

profile of v0, /device:TPU:0, one launch (start us, length us, event | category | flops | bytes accessed | tf_op | source)
XLA Modules:
  0.0 128.3 jit_solution(12888911284694200555)
XLA Ops:
  0.6 1.9 %copy.5.start_ref = f32[1024,64]{1,0:T(8,128)} copy(f32[1024,64]{0,1:T(8,128)} %param.4) | data formatting | bytes 524288 | tf_op args[1]
  2.6 123.2 %shard_map.50 = (f32[1024,64]{1,0:T(8,128)}, f32[1,1024]{1,0:T(1,128)}) custom-call(f32[1024,128]{1,0:T(8,128)} %points_ref.1, f32[1024,64]{1,0:T(8,128)} %copy.5.start_ref, s32[1,7]{1,0:T(1,128)} %mask_ref.1), custom_call_target="tpu_custom_call" | custom-call | tf_op jit(solution)/shard_map/pallas_call | solution.py:239
  125.7 0.0 copy-start
  125.7 1.9 %copy.6 = f32[1024,64]{0,1:T(8,128)} copy(f32[1024,64]{1,0:T(8,128)} %get-tuple-element.6) | data formatting | bytes 524288
  127.7 0.0 copy-done
  127.7 0.6 copy.8
Async XLA Ops:
  125.7 1.9 %copy-start = (f32[1,1024]{1,0:T(1,128)S(1)}, f32[1,1024]{1,0:T(1,128)}, u32[]{:S(2)}) copy-start(f32[1,1024]{1,0:T(1,128)} %get-tuple-element.5) | copy-start | bytes 12292
where the time goes:
time: 128 us
  Pallas kernels  123 us (96%)
  local copies, waits for them, and re-layouts  4.46 us (3%)
    pallas_call x1, Pallas kernels, per_device(): pl.pallas_call(functools.partial(kernel, rows_n, span), out_shape=(jax.Sh...  123 us
    unnamed x5, local copies, waits for them, and re-layouts  4.46 us

commit v1 on v0

--- a/solution.py
+++ b/solution.py
@@ -11,6 +11,7 @@
 STEPS = 2
 MESH = pl.DeviceIdType.MESH
 PAD = 16
+RANGE = 8.0
 
 
 def inverse_cholesky(gram):
@@ -63,12 +64,12 @@
     def _():
         pl.semaphore_signal(barrier, inc=1, device_id=(group, far_chip, other), device_id_type=MESH)
 
-    pts[span, 0:blk, :] = points_ref[...].astype(jnp.bfloat16)
+    pts[span, 0:blk, :] = jnp.round(points_ref[...] * (32767.0 / RANGE)).astype(jnp.int32).astype(jnp.int16)
     lane = lax.broadcasted_iota(jnp.int32, (PAD, feats), 1)
-    flags = jnp.where(lane == feats - 1, 1.0, 0.0)
+    flags = jnp.where(lane == feats - 1, 1, 0)
     for i in range(span):
-        flags = jnp.where(lane == i, mask_ref[0, i].astype(jnp.float32), flags)
-    pts[span, blk:blk + PAD, :] = flags.astype(jnp.bfloat16)
+        flags = jnp.where(lane == i, mask_ref[0, i], flags)
+    pts[span, blk:blk + PAD, :] = flags.astype(jnp.int16)
 
     pl.semaphore_wait(barrier, rows_n + has_far.astype(jnp.int32))
 
@@ -129,22 +130,34 @@
                 def _(d=d):
                     relay(buf, send, recv, d).wait_send()
 
-    near_f = pts[span, 0:blk, :].astype(jnp.float32).T
-    near_t[...] = near_f.astype(jnp.bfloat16)
+    def decode(coded):
+        return coded.astype(jnp.int32).astype(jnp.float32) * (RANGE / 32767.0)
+
+    def split(exact):
+        high = exact.astype(jnp.bfloat16)
+        return high, (exact - high.astype(jnp.float32)).astype(jnp.bfloat16)
+
+    near_f = decode(pts[span, 0:blk, :]).T
+    near_high, near_low = split(near_f)
+    near_t[0:feats] = near_high
+    near_t[feats:2 * feats] = near_high
+    near_t[2 * feats:3 * feats] = near_low
+    near_t[3 * feats:4 * feats] = near_low
     near_sq = -c2 * jnp.sum(near_f * near_f, axis=0, keepdims=True)
     degree_ref[...] = jnp.zeros_like(degree_ref)
     step = 128
 
     def make_tile(d):
-        flag_row = pts[span + jnp.minimum(d, 0), blk:blk + PAD, :].astype(jnp.float32)
+        flag_row = pts[span + jnp.minimum(d, 0), blk:blk + PAD, :].astype(jnp.int32).astype(jnp.float32)
         which = jnp.where(d == 0, feats - 1, jnp.abs(d) - 1)
         live = jnp.sum(jnp.where(lane == which, flag_row, 0.0)[0:1], axis=1, keepdims=True)
         near_term = near_sq + (1.0 - live) * -1.0e4
 
         def part(i, sums):
             at = pl.ds(pl.multiple_of(i * step, step), step)
-            far = pts[span + d, at, :]
-            far_f = far.astype(jnp.float32)
+            far_f = decode(pts[span + d, at, :])
+            far_high, far_low = split(far_f)
+            far = jnp.concatenate([far_high, far_low, far_high, far_low], axis=1)
             far_sq = -c2 * jnp.sum(far_f * far_f, axis=1, keepdims=True)
             inner = jnp.dot(far, near_t[...], preferred_element_type=jnp.float32)
             tile = jnp.exp2((2.0 * c2) * inner + far_sq + near_term).astype(jnp.bfloat16)
@@ -242,8 +255,8 @@
         in_specs=[vmem, vmem, pl.BlockSpec(memory_space=pltpu.SMEM)],
         out_specs=(vmem, vmem),
         scratch_shapes=[
-            pltpu.VMEM((slots, blk + PAD, feats), jnp.bfloat16),
-            pltpu.VMEM((feats, blk), jnp.bfloat16),
+            pltpu.VMEM((slots, blk + PAD, feats), jnp.int16),
+            pltpu.VMEM((4 * feats, blk), jnp.bfloat16),
             pltpu.VMEM((slots, blk, blk), jnp.bfloat16),
             pltpu.VMEM((STEPS, slots, width, blk), jnp.bfloat16),
             pltpu.VMEM((width, blk), jnp.float32),

time: 128 us -> 135 us (1.055)
  Pallas kernels: 123 us -> 130 us
    pallas_call x1, Pallas kernels: 123 us -> 130 us  [per_device(): pl.pallas_call(functools.partial(kernel, rows_n, span), out_shape=(jax.Sh...]
where the time goes in v1:
time: 135 us
  Pallas kernels  130 us (96%)
  local copies, waits for them, and re-layouts  4.46 us (3%)
    pallas_call x1, Pallas kernels, per_device(): pl.pallas_call(functools.partial(kernel, rows_n, span), out_shape=(jax.Sh...  130 us
    unnamed x5, local copies, waits for them, and re-layouts  4.46 us

profile of v1, /device:TPU:0, one launch (start us, length us, event | category | flops | bytes accessed | tf_op | source)
XLA Modules:
  0.0 135.0 jit_solution(13024943115891797517)
XLA Ops:
  0.6 1.9 %copy.5.start_ref = f32[1024,64]{1,0:T(8,128)} copy(f32[1024,64]{0,1:T(8,128)} %param.4) | data formatting | bytes 524288 | tf_op args[1]
  2.6 129.8 %shard_map.50 = (f32[1024,64]{1,0:T(8,128)}, f32[1,1024]{1,0:T(1,128)}) custom-call(f32[1024,128]{1,0:T(8,128)} %points_ref.1, f32[1024,64]{1,0:T(8,128)} %copy.5.start_ref, s32[1,7]{1,0:T(1,128)} %mask_ref.1), custom_call_target="tpu_custom_call" | custom-call | tf_op jit(solution)/shard_map/pallas_call | solution.py:252
  132.4 0.0 copy-start
  132.4 1.9 %copy.6 = f32[1024,64]{0,1:T(8,128)} copy(f32[1024,64]{1,0:T(8,128)} %get-tuple-element.6) | data formatting | bytes 524288
  134.4 0.0 copy-done
  134.4 0.6 copy.8
Async XLA Ops:
  132.4 1.9 %copy-start = (f32[1,1024]{1,0:T(1,128)S(1)}, f32[1,1024]{1,0:T(1,128)}, u32[]{:S(2)}) copy-start(f32[1,1024]{1,0:T(1,128)} %get-tuple-element.5) | copy-start | bytes 12292

commit v2 on v1

--- a/solution.py
+++ b/solution.py
@@ -16,24 +16,31 @@
 
 def inverse_cholesky(gram):
     n = gram.shape[0]
+    group = 4
     rows = lax.broadcasted_iota(jnp.int32, (n, 2 * n), 0)
     lanes = lax.broadcasted_iota(jnp.int32, (n, 2 * n), 1)
-    eye = jnp.where(lanes == rows + n, 1.0, 0.0)
-    mat = jnp.concatenate([gram, jnp.zeros_like(gram)], axis=1) + eye
-    diag = jnp.ones((n, 1), jnp.float32)
-    row_of = lax.broadcasted_iota(jnp.int32, (n, 1), 0)
-    for k in range(n):
-        pivot = mat[k:k + 1, k:k + 1]
-        diag = jnp.where(row_of == k, pivot, diag)
-        if k < n - 1:
-            line = mat[k:k + 1, :] * (1.0 / pivot)
-            column = jnp.where(row_of > k, mat[:, k:k + 1], 0.0)
-            mat = mat - column * line
-    return mat[:, n:] * lax.rsqrt(diag)
+    mat = jnp.concatenate([gram, jnp.zeros_like(gram)], axis=1) + jnp.where(lanes == rows + n, 1.0, 0.0)
+    done = []
+    for k in range(0, n, group):
+        lines = [mat[k + i:k + i + 1, :] for i in range(group)]
+        columns = [jnp.broadcast_to(mat[:, k + i:k + i + 1], (n, 2 * n)) for i in range(group)]
+        corner = [[columns[j][k + i:k + i + 1, :] for j in range(group)] for i in range(group)]
+        for i in range(group):
+            inverse = 1.0 / corner[i][i]
+            for j in range(i + 1, group):
+                ratio = corner[i][j] * inverse
+                for m in range(j, group):
+                    corner[j][m] = corner[j][m] - ratio * corner[i][m]
+                lines[j] = lines[j] - ratio * lines[i]
+                columns[j] = columns[j] - ratio * columns[i]
+            done.append(lines[i] * lax.rsqrt(corner[i][i]))
+            if k + group < n:
+                mat = mat - columns[i] * (lines[i] * inverse)
+    return jnp.concatenate(done, axis=0)[:, n:]
 
 
 def kernel(rows_n, span, points_ref, start_ref, mask_ref, out_ref, degree_ref,
-           pts, near_t, tiles, emb, acc, y_t, gram, gram_near, gram_all, gram_sum,
+           pts, near_t, far, tiles, emb, acc, y_t, gram, gram_near, gram_all, gram_sum,
            pts_send, pts_recv, emb_send, emb_recv, gsend, grecv, gall_send, gall_recv):
     group = lax.axis_index("groups")
     chip = lax.axis_index("row")
@@ -138,14 +145,14 @@
         return high, (exact - high.astype(jnp.float32)).astype(jnp.bfloat16)
 
     near_f = decode(pts[span, 0:blk, :]).T
-    near_high, near_low = split(near_f)
+    near_high, near_low = split((2.0 * c2) * near_f)
     near_t[0:feats] = near_high
     near_t[feats:2 * feats] = near_high
     near_t[2 * feats:3 * feats] = near_low
     near_t[3 * feats:4 * feats] = near_low
     near_sq = -c2 * jnp.sum(near_f * near_f, axis=0, keepdims=True)
     degree_ref[...] = jnp.zeros_like(degree_ref)
-    step = 128
+    step = min(256, blk)
 
     def make_tile(d):
         flag_row = pts[span + jnp.minimum(d, 0), blk:blk + PAD, :].astype(jnp.int32).astype(jnp.float32)
@@ -153,18 +160,18 @@
         live = jnp.sum(jnp.where(lane == which, flag_row, 0.0)[0:1], axis=1, keepdims=True)
         near_term = near_sq + (1.0 - live) * -1.0e4
 
-        def part(i, sums):
-            at = pl.ds(pl.multiple_of(i * step, step), step)
-            far_f = decode(pts[span + d, at, :])
-            far_high, far_low = split(far_f)
-            far = jnp.concatenate([far_high, far_low, far_high, far_low], axis=1)
-            far_sq = -c2 * jnp.sum(far_f * far_f, axis=1, keepdims=True)
-            inner = jnp.dot(far, near_t[...], preferred_element_type=jnp.float32)
-            tile = jnp.exp2((2.0 * c2) * inner + far_sq + near_term).astype(jnp.bfloat16)
-            tiles[span + d, at, :] = tile
-            return sums + jnp.sum(tile.astype(jnp.float32), axis=0, keepdims=True)
-
-        degree_ref[...] += lax.fori_loop(0, blk // step, part, jnp.zeros((1, blk), jnp.float32))
+        far_f = decode(pts[span + d, 0:blk, :])
+        far_sq = -c2 * jnp.sum(far_f * far_f, axis=1, keepdims=True)
+        far_high, far_low = split(far_f)
+        far[:, 0:feats] = far_high
+        far[:, feats:2 * feats] = far_low
+        for at in range(0, blk, step):
+            here = slice(at, at + step)
+            inner = (jnp.dot(far[...], near_t[0:2 * feats, here], preferred_element_type=jnp.float32)
+                     + jnp.dot(far[...], near_t[2 * feats:4 * feats, here], preferred_element_type=jnp.float32))
+            tile = jnp.exp2(inner + far_sq + near_term[:, here]).astype(jnp.bfloat16)
+            tiles[span + d, :, here] = tile
+            degree_ref[:, here] += jnp.sum(tile.astype(jnp.float32), axis=0, keepdims=True)
 
     exchange(pts, pts_send, pts_recv, make_tile)
     inverse_root = lax.rsqrt(degree_ref[...])
@@ -257,6 +264,7 @@
         scratch_shapes=[
             pltpu.VMEM((slots, blk + PAD, feats), jnp.int16),
             pltpu.VMEM((4 * feats, blk), jnp.bfloat16),
+            pltpu.VMEM((blk, 2 * feats), jnp.bfloat16),
             pltpu.VMEM((slots, blk, blk), jnp.bfloat16),
             pltpu.VMEM((STEPS, slots, width, blk), jnp.bfloat16),
             pltpu.VMEM((width, blk), jnp.float32),

time: 135 us -> 110 us (0.81)
  Pallas kernels: 130 us -> 105 us
    pallas_call x1, Pallas kernels: 130 us -> 105 us  [per_device(): pl.pallas_call(functools.partial(kernel, rows_n, span), out_shape=(jax.Sh...]
where the time goes in v2:
time: 110 us
  Pallas kernels  105 us (95%)
  local copies, waits for them, and re-layouts  4.46 us (4%)
    pallas_call x1, Pallas kernels, per_device(): pl.pallas_call(functools.partial(kernel, rows_n, span), out_shape=(jax.Sh...  105 us
    unnamed x5, local copies, waits for them, and re-layouts  4.46 us

profile of v2, /device:TPU:0, one launch (start us, length us, event | category | flops | bytes accessed | tf_op | source)
XLA Modules:
  0.0 110.3 jit_solution(448970721270167040)
XLA Ops:
  0.6 1.9 %copy.5.start_ref = f32[1024,64]{1,0:T(8,128)} copy(f32[1024,64]{0,1:T(8,128)} %param.4) | data formatting | bytes 524288 | tf_op args[1]
  2.6 105.2 %shard_map.50 = (f32[1024,64]{1,0:T(8,128)}, f32[1,1024]{1,0:T(1,128)}) custom-call(f32[1024,128]{1,0:T(8,128)} %points_ref.1, f32[1024,64]{1,0:T(8,128)} %copy.5.start_ref, s32[1,7]{1,0:T(1,128)} %mask_ref.1), custom_call_target="tpu_custom_call" | custom-call | tf_op jit(solution)/shard_map/pallas_call | solution.py:259
  107.8 0.0 copy-start
  107.8 1.9 %copy.6 = f32[1024,64]{0,1:T(8,128)} copy(f32[1024,64]{1,0:T(8,128)} %get-tuple-element.6) | data formatting | bytes 524288
  109.7 0.0 copy-done
  109.7 0.6 copy.8
Async XLA Ops:
  107.8 1.9 %copy-start = (f32[1,1024]{1,0:T(1,128)S(1)}, f32[1,1024]{1,0:T(1,128)}, u32[]{:S(2)}) copy-start(f32[1,1024]{1,0:T(1,128)} %get-tuple-element.5) | copy-start | bytes 12292

commit v3 on v2

--- a/solution.py
+++ b/solution.py
@@ -112,6 +112,9 @@
             r = (t + 3) % 4
             size = jnp.minimum(jnp.where(r < 2, 2 * g + 2, 2 * g + 1), span)
             d = jnp.where(t == 0, 0, jnp.where(r % 2 == 0, size, -size))
+            d = jnp.where(t == 1, side, jnp.where(t == 4, -side, d))
+            d = jnp.where(t == 2, 2, jnp.where(t == 3, -2, d))
+            size = jnp.abs(d)
             valid = jnp.logical_and(mine + d >= 0, mine + d < total)
 
             @pl.when(jnp.logical_and(valid, d != 0))

time: 110 us -> 109 us (level)
  Pallas kernels: 105 us -> 103 us
    pallas_call x1, Pallas kernels: 105 us -> 103 us  [per_device(): pl.pallas_call(functools.partial(kernel, rows_n, span), out_shape=(jax.Sh...]
where the time goes in v3:
time: 109 us; the launch traced here: 108 us
  Pallas kernels  103 us (94%)
  local copies, waits for them, and re-layouts  4.46 us (4%)
    pallas_call x1, Pallas kernels, per_device(): pl.pallas_call(functools.partial(kernel, rows_n, span), out_shape=(jax.Sh...  103 us
    unnamed x5, local copies, waits for them, and re-layouts  4.46 us

profile of v3, /device:TPU:0, one launch (start us, length us, event | category | flops | bytes accessed | tf_op | source)
XLA Modules:
  0.0 108.3 jit_solution(382644640364401238)
XLA Ops:
  0.6 1.9 %copy.5.start_ref = f32[1024,64]{1,0:T(8,128)} copy(f32[1024,64]{0,1:T(8,128)} %param.4) | data formatting | bytes 524288 | tf_op args[1]
  2.6 103.2 %shard_map.50 = (f32[1024,64]{1,0:T(8,128)}, f32[1,1024]{1,0:T(1,128)}) custom-call(f32[1024,128]{1,0:T(8,128)} %points_ref.1, f32[1024,64]{1,0:T(8,128)} %copy.5.start_ref, s32[1,7]{1,0:T(1,128)} %mask_ref.1), custom_call_target="tpu_custom_call" | custom-call | tf_op jit(solution)/shard_map/pallas_call | solution.py:262
  105.8 0.0 copy-start
  105.8 1.9 %copy.6 = f32[1024,64]{0,1:T(8,128)} copy(f32[1024,64]{1,0:T(8,128)} %get-tuple-element.6) | data formatting | bytes 524288
  107.7 0.0 copy-done
  107.7 0.6 copy.8
Async XLA Ops:
  105.8 1.9 %copy-start = (f32[1,1024]{1,0:T(1,128)S(1)}, f32[1,1024]{1,0:T(1,128)}, u32[]{:S(2)}) copy-start(f32[1,1024]{1,0:T(1,128)} %get-tuple-element.5) | copy-start | bytes 12292
